TPU v7x, 512 devices: a whole 4x4x16 slice. The times are simulated.
512 devices in a mesh: chan: 64 (over z, y), rad: 8 (over x, core).
Axes of the slice: x: 4, y: 4, z: 16, core: 2. Of those that a mesh axis runs over, the one named last changes fastest.
Arguments:
- trial_block: float32 [1024, 16, 128], P('chan', None, 'rad')
- ham_blocks: bfloat16 [1024, 8, 128, 128], P('chan', None, 'rad'), may hold values from -0.1875 to 0.1875
- partners: int32 [1024, 8], P('chan'), may hold values from 0 to 1023, as said below
- stored_at: int32 [1024], replicated, may hold values from 0 to 1023, as said below
- precond_diag: float32 [1024, 128], P('chan', 'rad'), may hold values from 1 to 10
Outputs:
- new_block: float32 [1024, 16, 128], P('chan', None, 'rad')
- ritz_values: float32 [16], replicated
Inputs may be any that keep to these rules, and one draw needn't show every extreme that they name: `stored_at`: A permutation of the channel numbers. `partners`: among the 128 entries of the rows p with p // 16 = d, for every d, at most 4 have stored_at[partner] // 16 equal to any one value; for every d some value has exactly 4.
All inputs are finite; a program needn't handle non-finite values.
Results may differ from a plain program's by a relative error of at most 0.0051.
Values may be sent and summed in bfloat16 or wider, within the bound.
A program may use at most 64 MiB of HBM per device.

v0:
```python
import jax
import jax.numpy as jnp
from jax import lax
from jax.sharding import PartitionSpec as P

NCH = 1024
NB = 128


def chol_solve(factor, rhs):
    first = lax.linalg.triangular_solve(factor, rhs, left_side=True, lower=True)
    return lax.linalg.triangular_solve(factor, first, left_side=True, lower=True, transpose_a=True)


def inner_products(left, right):
    return jnp.einsum("pkr,plr->kl", left, right, precision=lax.Precision.HIGHEST)


def body(trial_block, ham_blocks, partners, stored_at, precond_diag):
    n_chan = lax.axis_size("chan")
    ch_dev = trial_block.shape[0]
    vectors = trial_block.shape[1]
    ncoup = partners.shape[1]
    capacity = 2 * ch_dev * ncoup // n_chan
    stored_rows = jnp.take(stored_at, partners.reshape(-1))
    owner_dev = stored_rows // ch_dev
    local_row = stored_rows % ch_dev
    one_hot = (owner_dev[:, None] == jnp.arange(n_chan, dtype=jnp.int32)[None, :]).astype(jnp.int32)
    running = jnp.cumsum(one_hot, axis=0)
    order_rank = jnp.sum(running * one_hot, axis=1) - 1
    slot_index = owner_dev * capacity + order_rank
    wanted = (
        jnp.zeros((n_chan * capacity,), jnp.int32)
        .at[slot_index]
        .set(local_row)
        .reshape(n_chan, capacity)
    )
    asked = lax.all_to_all(wanted, "chan", split_axis=0, concat_axis=0, tiled=True)
    rounded = trial_block.astype(jnp.bfloat16)
    whole_rows = lax.all_gather(rounded, "rad", axis=2, tiled=True)
    served = whole_rows[asked]
    received = lax.all_to_all(served, "chan", split_axis=0, concat_axis=0, tiled=True)
    full_splines = received.shape[3]
    coupled = received.reshape(n_chan * capacity, vectors, full_splines)[slot_index]
    coupled = coupled.reshape(ch_dev, ncoup, vectors, full_splines)
    applied = lax.dot_general(
        coupled, ham_blocks, (((1, 3), (1, 3)), ((0,), (0,))), preferred_element_type=jnp.float32
    )
    total_rows = jnp.float32(NCH * NB)
    proj_a, proj_b = lax.psum(
        (inner_products(trial_block, applied), inner_products(trial_block, trial_block)),
        ("chan", "rad"),
    )
    factor = jnp.linalg.cholesky(proj_b)
    coefficients = chol_solve(factor, proj_a)
    ritz_values = jnp.diagonal(coefficients)
    residual = applied - jnp.einsum(
        "pkr,kl->plr", trial_block, coefficients, precision=lax.Precision.HIGHEST
    )
    correction = residual / precond_diag[:, None, :]
    correlation = lax.psum(inner_products(trial_block, correction), ("chan", "rad"))
    mixing = chol_solve(factor, correlation)
    projected = correction - jnp.einsum(
        "pkr,kl->plr", trial_block, mixing, precision=lax.Precision.HIGHEST
    )
    correlation_gram = lax.psum(inner_products(projected, projected), ("chan", "rad")) / total_rows
    gram_factor = jnp.linalg.cholesky(correlation_gram)
    local_splines = projected.shape[2]
    flat_rows = jnp.transpose(projected, (1, 0, 2)).reshape(vectors, -1)
    solved = lax.linalg.triangular_solve(gram_factor, flat_rows, left_side=True, lower=True)
    new_block = jnp.transpose(solved.reshape(vectors, ch_dev, local_splines), (1, 0, 2))
    return (new_block, ritz_values)


def solution(mesh):
    return jax.shard_map(
        body,
        mesh=mesh,
        in_specs=(
            P("chan", None, "rad"),
            P("chan", None, "rad", None),
            P("chan", None),
            P(),
            P("chan", "rad"),
        ),
        out_specs=(P("chan", None, "rad"), P()),
        check_vma=False,
    )
```

profile of v0, /device:TPU:1, one launch (start us, length us, event | category | flops | bytes accessed | tf_op | source)
XLA Modules:
  0.0 426.4 jit_solution(2646082566353192529)
XLA Ops:
  0.6 0.8 copy.36
  1.5 0.1 reshape.211
  1.5 0.1 reshape.212
  1.7 0.7 copy-done.1
  2.3 1.0 gather_fusion
  3.3 0.1 fusion.4
  3.4 0.2 reduce_window_sum.11
  3.6 0.2 select_reduce_fusion
  3.8 1.0 scatter_custom_fusion
  4.8 0.7 all_to_all.11
  5.5 19.3 %all-to-all-start = ((s32[64,1,4]{2,1,0:T(1,128)}), s32[64,1,4]{2,1,0:T(1,128)S(1)}, u32[]{:S(2)}, u32[]{:S(2)}) async-start(s32[64,1,4]{2,1,0:T(1,128)} %bitcast.4), calls=%async_computation | async-start | bytes 65536 | tf_op jit(solution)/shard_map/all_to_all | solution.py:38
  24.8 0.1 copy.35
  24.9 14.3 %all_gather.3 = bf16[16,16,128]{1,0,2:T(8,128)(2,1)S(1)} all-gather(bf16[16,16,16]{1,0,2:T(8,128)(2,1)S(1)} %copy.35), channel_id=1, replica_groups=mesh['chan'=64,'rad'=8] {'rad'}, dimensions={2}, use_global_device_ids=true | all-gather | bytes 73728 | tf_op jit(solution)/shard_map/all_gather | solution.py:40
  39.2 0.4 copy.39
  39.6 0.1 reshape.230
  39.8 1.8 gather_fusion.1
  41.5 14.8 %all-to-all-start.1 = ((bf16[64,4,16,128]{3,2,1,0:T(8,128)(2,1)}), bf16[64,4,16,128]{3,2,1,0:T(8,128)(2,1)S(1)}, u32[]{:S(2)}, u32[]{:S(2)}) async-start(bf16[64,4,16,128]{3,2,1,0:T(8,128)(2,1)} %bitcast.6), calls=%async_computation.1 | async-start | bytes 2097152 | tf_op jit(solution)/shard_map/all_to_all | solution.py:42
  56.4 0.2 convolution_bitcast_fusion.5
  56.6 52.5 %all-to-all-done.1 = bf16[64,4,16,128]{3,2,1,0:T(8,128)(2,1)S(1)} async-done(((bf16[64,4,16,128]{3,2,1,0:T(8,128)(2,1)}), bf16[64,4,16,128]{3,2,1,0:T(8,128)(2,1)S(1)}, u32[]{:S(2)}, u32[]{:S(2)}) %all-to-all-start.1) | async-done | bytes 1048608 | tf_op jit(solution)/shard_map/all_to_all | solution.py:42
  109.2 0.7 gather_fusion.2
  109.9 0.3 fusion.27
  110.2 0.3 convolution_bitcast_fusion.4
  110.4 103.4 %all-reduce = (f32[16,16]{0,1:T(8,128)S(1)}, f32[16,16]{0,1:T(8,128)S(1)}) all-reduce(f32[16,16]{0,1:T(8,128)S(1)} %convolution_bitcast_fusion.4, f32[16,16]{0,1:T(8,128)S(1)} %convolution_bitcast_fusion.5), channel_id=1, replica_groups=mesh['chan'=64,'rad'=8] {'chan','rad'}, use_global_device_ids=true, to_apply=%region_6.8 | all-reduce | flops 512 | bytes 4096 | tf_op jit(solution)/shard_map/psum | solution.py:50
  213.8 0.1 copy.41
  213.9 1.5 cholesky.44
  215.4 0.6 compare_reduce_fusion.1
  216.0 0.6 fusion.5
  216.7 1.2 custom-call.17
  217.9 0.2 fusion.14
  218.1 0.1 fusion.16
  218.3 0.3 fusion.9
  218.6 0.4 copy-done.3
  219.0 0.3 convolution_bitcast_fusion.3
  219.3 99.6 %psum.30 = f32[16,16]{0,1:T(8,128)S(1)} all-reduce(f32[16,16]{0,1:T(8,128)S(1)} %convolution_bitcast_fusion.3), channel_id=1, replica_groups=mesh['chan'=64,'rad'=8] {'chan','rad'}, use_global_device_ids=true, to_apply=%region_7.11 | all-reduce | flops 256 | bytes 2048 | tf_op jit(solution)/shard_map/psum | solution.py:61
  318.9 0.2 fusion.11
  319.1 0.2 convolution_bitcast_fusion.2
  319.3 0.3 fusion.1
  319.6 0.3 convolution_bitcast_fusion.1
  319.8 99.4 %psum.31 = f32[16,16]{0,1:T(8,128)S(1)} all-reduce(f32[16,16]{0,1:T(8,128)S(1)} %convolution_bitcast_fusion.1), channel_id=1, replica_groups=mesh['chan'=64,'rad'=8] {'chan','rad'}, use_global_device_ids=true, to_apply=%region_8.12 | all-reduce | flops 256 | bytes 2048 | tf_op jit(solution)/shard_map/psum | solution.py:66
  419.2 0.1 copy.44
  419.2 1.5 cholesky.55
  420.7 0.6 compare_reduce_fusion
  421.4 0.6 fusion.6
  422.0 1.2 custom-call.11
  423.3 0.1 reshape.215
  423.4 0.1 copy.56
  423.5 1.2 gather_fusion.3
  424.7 1.7 convolution_bitcast_fusion
  (22 shorter events, 0.2 us)
Async XLA Ops:
  0.6 109.2 %copy-start = (bf16[16,8,16,128]{3,2,1,0:T(8,128)(2,1)S(1)}, bf16[16,8,16,128]{3,2,1,0:T(8,128)(2,1)}, u32[]{:S(2)}) copy-start(bf16[16,8,16,128]{3,2,1,0:T(8,128)(2,1)} %param.11) | copy-start | bytes 1572868
  1.6 0.7 copy-start.1
  3.4 21.4 %copy-start.2 = (f32[16,16,16]{2,1,0:T(8,128)S(1)}, f32[16,16,16]{2,1,0:T(8,128)}, u32[]{:S(2)}) copy-start(f32[16,16,16]{2,1,0:T(8,128)} %param.10) | copy-start | bytes 49156
  5.5 34.1 %all-to-all-start = ((s32[64,1,4]{2,1,0:T(1,128)}), s32[64,1,4]{2,1,0:T(1,128)S(1)}, u32[]{:S(2)}, u32[]{:S(2)}) async-start(s32[64,1,4]{2,1,0:T(1,128)} %bitcast.4), calls=%async_computation | async-start | bytes 65536 | tf_op jit(solution)/shard_map/all_to_all | solution.py:38
  41.5 67.6 %all-to-all-start.1 = ((bf16[64,4,16,128]{3,2,1,0:T(8,128)(2,1)}), bf16[64,4,16,128]{3,2,1,0:T(8,128)(2,1)S(1)}, u32[]{:S(2)}, u32[]{:S(2)}) async-start(bf16[64,4,16,128]{3,2,1,0:T(8,128)(2,1)} %bitcast.6), calls=%async_computation.1 | async-start | bytes 2097152 | tf_op jit(solution)/shard_map/all_to_all | solution.py:42
  218.3 0.7 copy-start.3
where the time goes:
time: 427 us; the launch traced here: 426 us
  blocking collectives  317 us (74%)
  waiting for transfers between devices  52.5 us (12%)
  starting transfers between devices  34.1 us (8%)
  local copies, waits for them, and re-layouts  9.41 us (2%)
  other arithmetic  8.53 us (2%)
  matrix products  4.37 us (1%)
    psum x1, blocking collectives, body(): lax.psum((inner_products(trial_block, applied), inner_products(trial_bloc...  103 us
    psum x1, blocking collectives, body(): lax.psum(inner_products(trial_block, correction), ('chan', 'rad'))  99.6 us
    psum x1, blocking collectives, body(): lax.psum(inner_products(projected, projected), ('chan', 'rad')) / total_rows  99.4 us
    all_to_all x1, waiting for transfers between devices, body(): lax.all_to_all(served, 'chan', split_axis=0, concat_axis=0, tiled=True)  52.5 us
    all_to_all x1, starting transfers between devices, body(): lax.all_to_all(wanted, 'chan', split_axis=0, concat_axis=0, tiled=True)  19.3 us
    all_to_all x1, starting transfers between devices, body(): lax.all_to_all(served, 'chan', split_axis=0, concat_axis=0, tiled=True)  14.8 us
    all_gather x1, blocking collectives, body(): whole_rows = lax.all_gather(rounded, 'rad', axis=2, tiled=True)  14.3 us
  transfers between devices with their start and end apart: 2, of which 1 were waited for; matrix products, arithmetic and copies ran while one was open for 0% of the time, Pallas kernels for 0%

commit v1 on v0

--- a/solution.py
+++ b/solution.py
@@ -37,7 +37,16 @@
     )
     asked = lax.all_to_all(wanted, "chan", split_axis=0, concat_axis=0, tiled=True)
     rounded = trial_block.astype(jnp.bfloat16)
-    whole_rows = lax.all_gather(rounded, "rad", axis=2, tiled=True)
+    ways = lax.axis_size("rad")
+    up = [(d, (d + 1) % ways) for d in range(ways)]
+    down = [(d, (d - 1) % ways) for d in range(ways)]
+    earlier, later = ([rounded], [rounded])
+    for _ in range(ways // 2):
+        earlier.append(lax.ppermute(earlier[-1], "rad", up))
+    for _ in range((ways - 1) // 2):
+        later.append(lax.ppermute(later[-1], "rad", down))
+    line = jnp.concatenate([*earlier[::-1], *later[1:]], axis=2)
+    whole_rows = jnp.roll(line, (lax.axis_index("rad") - ways // 2) * rounded.shape[2], axis=2)
     served = whole_rows[asked]
     received = lax.all_to_all(served, "chan", split_axis=0, concat_axis=0, tiled=True)
     full_splines = received.shape[3]

time: 427 us -> 426 us (level)
  blocking collectives: 317 us -> 308 us
  waiting for transfers between devices: 52.5 us -> 61.3 us
    all_gather x1 -> x0, blocking collectives: 14.3 us -> none  [body(): whole_rows = lax.all_gather(rounded, 'rad', axis=2, tiled=True)]
    all_to_all x1, waiting for transfers between devices: 0.01 us -> 11.6 us  [body(): lax.all_to_all(wanted, 'chan', split_axis=0, concat_axis=0, tiled=True)]
    ppermute x0 -> x7, starting transfers between devices: none -> 10.4 us  [the longest x3 6.49 us: body(): later.append(lax.ppermute(later[-1], 'rad', down))]
    all_to_all x1, starting transfers between devices: 14.8 us -> 5.99 us  [body(): lax.all_to_all(served, 'chan', split_axis=0, concat_axis=0, tiled=True)]
    psum x1, blocking collectives: 103 us -> 110 us  [body(): lax.psum((inner_products(trial_block, applied), inner_products(trial_bloc...]
    all_to_all x1, waiting for transfers between devices: 52.5 us -> 47.5 us  [body(): lax.all_to_all(served, 'chan', split_axis=0, concat_axis=0, tiled=True)]
  transfers between devices with their start and end apart: 2 -> 9, of which waited for: 1 -> 4; matrix products, arithmetic and copies ran while one was open for 0% -> 1% of each run, Pallas kernels for 0% -> 0%
where the time goes in v1:
time: 426 us; the launch traced here: 425 us
  blocking collectives  308 us (72%)
  waiting for transfers between devices  61.3 us (14%)
  starting transfers between devices  32.3 us (8%)
  other arithmetic  9.5 us (2%)
  local copies, waits for them, and re-layouts  8.72 us (2%)
  matrix products  4.37 us (1%)
    psum x1, blocking collectives, body(): lax.psum((inner_products(trial_block, applied), inner_products(trial_bloc...  110 us
    psum x1, blocking collectives, body(): lax.psum(inner_products(trial_block, correction), ('chan', 'rad'))  99.5 us
    psum x1, blocking collectives, body(): lax.psum(inner_products(projected, projected), ('chan', 'rad')) / total_rows  98.9 us
    all_to_all x1, waiting for transfers between devices, body(): lax.all_to_all(served, 'chan', split_axis=0, concat_axis=0, tiled=True)  47.5 us
    all_to_all x1, starting transfers between devices, body(): lax.all_to_all(wanted, 'chan', split_axis=0, concat_axis=0, tiled=True)  15.9 us
    all_to_all x1, waiting for transfers between devices, body(): lax.all_to_all(wanted, 'chan', split_axis=0, concat_axis=0, tiled=True)  11.6 us
  transfers between devices with their start and end apart: 9, of which 4 were waited for; matrix products, arithmetic and copies ran while one was open for 1% of the time, Pallas kernels for 0%

profile of v1, /device:TPU:1, one launch (start us, length us, event | category | flops | bytes accessed | tf_op | source)
XLA Modules:
  0.0 425.4 jit_solution(5706979636330114517)
XLA Ops:
  0.7 1.0 convert_element_type.6
  1.6 2.6 collective-permute-start
  4.2 4.3 %collective-permute-start.4 = (bf16[16,16,16]{2,1,0:T(8,128)(2,1)S(1)}, bf16[16,16,16]{2,1,0:T(8,128)(2,1)S(1)}, u32[]{:S(2)}, u32[]{:S(2)}) collective-permute-start(bf16[16,16,16]{2,1,0:T(8,128)(2,1)S(1)} %convert_element_type.6), channel_id=1, source_target_pairs={{0,7},{1,0},{2,1},{3,2},{4,3},{5,4},{6,5},{7,6},{8,15},{9,8},{10,9... | collective-permute-start | bytes 24584 | tf_op jit(solution)/shard_map/ppermute | solution.py:47
  8.8 0.7 copy-done.1
  9.5 1.0 gather_fusion
  10.6 0.2 reduce_window_sum.11
  10.8 0.2 select_reduce_fusion
  11.0 1.0 scatter_custom_fusion
  12.0 0.7 all_to_all.11
  12.7 15.9 %all-to-all-start = ((s32[64,1,4]{2,1,0:T(1,128)}), s32[64,1,4]{2,1,0:T(1,128)S(1)}, u32[]{:S(2)}, u32[]{:S(2)}) async-start(s32[64,1,4]{2,1,0:T(1,128)} %bitcast.4), calls=%async_computation | async-start | bytes 65536 | tf_op jit(solution)/shard_map/all_to_all | solution.py:38
  28.6 0.4 collective-permute-start.5
  29.1 1.3 collective-permute-start.2
  30.4 11.6 %all-to-all-done = s32[64,1,4]{2,1,0:T(1,128)S(1)} async-done(((s32[64,1,4]{2,1,0:T(1,128)}), s32[64,1,4]{2,1,0:T(1,128)S(1)}, u32[]{:S(2)}, u32[]{:S(2)}) %all-to-all-start) | async-done | bytes 1056 | tf_op jit(solution)/shard_map/all_to_all | solution.py:38
  42.0 0.1 reshape.230
  42.1 1.8 collective-permute-start.6
  43.9 1.9 collective-permute-done.6
  45.8 0.2 collective-permute-done.3
  46.0 0.5 concatenate.10
  46.6 1.8 gather_fusion.1
  48.4 6.0 %all-to-all-start.1 = ((bf16[64,4,16,128]{3,2,1,0:T(8,128)(2,1)}), bf16[64,4,16,128]{3,2,1,0:T(8,128)(2,1)S(1)}, u32[]{:S(2)}, u32[]{:S(2)}) async-start(bf16[64,4,16,128]{3,2,1,0:T(8,128)(2,1)} %bitcast.6), calls=%async_computation.1 | async-start | bytes 2097152 | tf_op jit(solution)/shard_map/all_to_all | solution.py:51
  54.5 0.2 convolution_bitcast_fusion.5
  54.7 47.5 %all-to-all-done.1 = bf16[64,4,16,128]{3,2,1,0:T(8,128)(2,1)S(1)} async-done(((bf16[64,4,16,128]{3,2,1,0:T(8,128)(2,1)}), bf16[64,4,16,128]{3,2,1,0:T(8,128)(2,1)S(1)}, u32[]{:S(2)}, u32[]{:S(2)}) %all-to-all-start.1) | async-done | bytes 1048608 | tf_op jit(solution)/shard_map/all_to_all | solution.py:51
  102.2 0.7 gather_fusion.2
  102.9 0.3 fusion.27
  103.2 0.3 convolution_bitcast_fusion.4
  103.5 109.9 %all-reduce = (f32[16,16]{0,1:T(8,128)S(1)}, f32[16,16]{0,1:T(8,128)S(1)}) all-reduce(f32[16,16]{0,1:T(8,128)S(1)} %convolution_bitcast_fusion.4, f32[16,16]{0,1:T(8,128)S(1)} %convolution_bitcast_fusion.5), channel_id=1, replica_groups=mesh['chan'=64,'rad'=8] {'chan','rad'}, use_global_device_ids=true, to_apply=%region_6.8 | all-reduce | flops 512 | bytes 4096 | tf_op jit(solution)/shard_map/psum | solution.py:59
  213.5 1.5 cholesky.44
  215.0 0.6 compare_reduce_fusion.1
  215.6 0.6 fusion.5
  216.3 1.2 custom-call.17
  217.5 0.2 fusion.14
  217.7 0.1 fusion.16
  217.8 0.3 fusion.9
  218.2 0.4 copy-done.3
  218.5 0.3 convolution_bitcast_fusion.3
  218.8 99.5 %psum.30 = f32[16,16]{0,1:T(8,128)S(1)} all-reduce(f32[16,16]{0,1:T(8,128)S(1)} %convolution_bitcast_fusion.3), channel_id=1, replica_groups=mesh['chan'=64,'rad'=8] {'chan','rad'}, use_global_device_ids=true, to_apply=%region_7.11 | all-reduce | flops 256 | bytes 2048 | tf_op jit(solution)/shard_map/psum | solution.py:70
  318.3 0.2 fusion.11
  318.5 0.2 convolution_bitcast_fusion.2
  318.7 0.3 fusion.1
  319.0 0.3 convolution_bitcast_fusion.1
  319.2 98.9 %psum.31 = f32[16,16]{0,1:T(8,128)S(1)} all-reduce(f32[16,16]{0,1:T(8,128)S(1)} %convolution_bitcast_fusion.1), channel_id=1, replica_groups=mesh['chan'=64,'rad'=8] {'chan','rad'}, use_global_device_ids=true, to_apply=%region_8.12 | all-reduce | flops 256 | bytes 2048 | tf_op jit(solution)/shard_map/psum | solution.py:75
  418.2 1.5 cholesky.55
  419.7 0.6 compare_reduce_fusion
  420.4 0.6 fusion.6
  421.0 1.2 custom-call.11
  422.3 0.1 reshape.215
  422.5 1.2 gather_fusion.3
  423.7 1.7 convolution_bitcast_fusion
  (38 shorter events, 0.9 us)
Async XLA Ops:
  0.6 102.3 %copy-start = (bf16[16,8,16,128]{3,2,1,0:T(8,128)(2,1)S(1)}, bf16[16,8,16,128]{3,2,1,0:T(8,128)(2,1)}, u32[]{:S(2)}) copy-start(bf16[16,8,16,128]{3,2,1,0:T(8,128)(2,1)} %param.11) | copy-start | bytes 1572868
  0.6 7.9 %copy-start.4 = (s32[16,8]{0,1:T(8,128)S(1)}, s32[16,8]{0,1:T(8,128)}, u32[]{:S(2)}) copy-start(s32[16,8]{0,1:T(8,128)} %param.12) | copy-start | bytes 1540
  1.6 9.3 %collective-permute-start = (bf16[16,16,16]{2,1,0:T(8,128)(2,1)S(1)}, bf16[16,16,16]{2,1,0:T(8,128)(2,1)S(1)}, u32[]{:S(2)}, u32[]{:S(2)}) collective-permute-start(bf16[16,16,16]{2,1,0:T(8,128)(2,1)S(1)} %convert_element_type.6), channel_id=1, source_target_pairs={{0,1},{1,2},{2,3},{3,4},{4,5},{5,6},{6,7},{7,0},{8,9},{9,10},{10,1... | collective-permute-start | bytes 24584 | tf_op jit(solution)/shard_map/ppermute | solution.py:45
  4.2 24.4 %collective-permute-start.4 = (bf16[16,16,16]{2,1,0:T(8,128)(2,1)S(1)}, bf16[16,16,16]{2,1,0:T(8,128)(2,1)S(1)}, u32[]{:S(2)}, u32[]{:S(2)}) collective-permute-start(bf16[16,16,16]{2,1,0:T(8,128)(2,1)S(1)} %convert_element_type.6), channel_id=1, source_target_pairs={{0,7},{1,0},{2,1},{3,2},{4,3},{5,4},{6,5},{7,6},{8,15},{9,8},{10,9... | collective-permute-start | bytes 24584 | tf_op jit(solution)/shard_map/ppermute | solution.py:47
  8.8 0.7 copy-start.1
  11.0 18.1 %collective-permute-start.1 = (bf16[16,16,16]{2,1,0:T(8,128)(2,1)S(1)}, bf16[16,16,16]{2,1,0:T(8,128)(2,1)S(1)}, u32[]{:S(2)}, u32[]{:S(2)}) collective-permute-start(bf16[16,16,16]{2,1,0:T(8,128)(2,1)S(1)} %collective-permute-done), channel_id=1, source_target_pairs={{0,1},{1,2},{2,3},{3,4},{4,5},{5,6},{6,7},{7,0},{8,9},{9,10},{10,1... | collective-permute-start | bytes 24584 | tf_op jit(solution)/shard_map/ppermute | solution.py:45
  12.7 29.3 %all-to-all-start = ((s32[64,1,4]{2,1,0:T(1,128)}), s32[64,1,4]{2,1,0:T(1,128)S(1)}, u32[]{:S(2)}, u32[]{:S(2)}) async-start(s32[64,1,4]{2,1,0:T(1,128)} %bitcast.4), calls=%async_computation | async-start | bytes 65536 | tf_op jit(solution)/shard_map/all_to_all | solution.py:38
  28.6 13.5 %collective-permute-start.5 = (bf16[16,16,16]{2,1,0:T(8,128)(2,1)S(1)}, bf16[16,16,16]{2,1,0:T(8,128)(2,1)S(1)}, u32[]{:S(2)}, u32[]{:S(2)}) collective-permute-start(bf16[16,16,16]{2,1,0:T(8,128)(2,1)S(1)} %collective-permute-done.4), channel_id=1, source_target_pairs={{0,7},{1,0},{2,1},{3,2},{4,3},{5,4},{6,5},{7,6},{8,15},{9,8},{10,9... | collective-permute-start | bytes 24584 | tf_op jit(solution)/shard_map/ppermute | solution.py:47
  29.1 14.8 %collective-permute-start.2 = (bf16[16,16,16]{2,1,0:T(8,128)(2,1)S(1)}, bf16[16,16,16]{2,1,0:T(8,128)(2,1)S(1)}, u32[]{:S(2)}, u32[]{:S(2)}) collective-permute-start(bf16[16,16,16]{2,1,0:T(8,128)(2,1)S(1)} %collective-permute-done.1), channel_id=1, source_target_pairs={{0,1},{1,2},{2,3},{3,4},{4,5},{5,6},{6,7},{7,0},{8,9},{9,10},{10,1... | collective-permute-start | bytes 24584 | tf_op jit(solution)/shard_map/ppermute | solution.py:45
  42.1 3.7 collective-permute-start.6
  43.8 2.2 collective-permute-start.3
  48.4 6.0 %copy-start.2 = (f32[16,16,16]{2,1,0:T(8,128)S(1)}, f32[16,16,16]{2,1,0:T(8,128)}, u32[]{:S(2)}) copy-start(f32[16,16,16]{2,1,0:T(8,128)} %param.10) | copy-start | bytes 49156
  48.4 53.8 %all-to-all-start.1 = ((bf16[64,4,16,128]{3,2,1,0:T(8,128)(2,1)}), bf16[64,4,16,128]{3,2,1,0:T(8,128)(2,1)S(1)}, u32[]{:S(2)}, u32[]{:S(2)}) async-start(bf16[64,4,16,128]{3,2,1,0:T(8,128)(2,1)} %bitcast.6), calls=%async_computation.1 | async-start | bytes 2097152 | tf_op jit(solution)/shard_map/all_to_all | solution.py:51
  217.8 0.7 copy-start.3
